TPU v7x, 256 devices: a whole 4x4x8 slice. The times are simulated.
256 devices in a mesh: front: 2 (over core), row: 16 (over y, x), col: 8 (over z).
Axes of the slice: x: 4, y: 4, z: 8, core: 2. Of those that a mesh axis runs over, the one named last changes fastest.
Arguments:
- children: float32 [2, 12288, 12288], P('front', 'row', 'col'), as said below
- pivot_inverse: bfloat16 [2, 3, 1024, 1024], P('front', None, 'row'), as said below
- parent_front: float32 [12288, 12288], P(('front', 'row'), 'col'), may hold values from -1.5 to 1.5
- child_map: int32 [2, 9216], replicated, may hold values from 0 to 12287, as said below
Outputs:
- parent_out: float32 [12288, 12288], P(('front', 'row'), 'col')
- factor: bfloat16 [2, 12288, 3072], P('front', 'row', 'col')
Inputs may be any that keep to these rules, and one draw needn't show every extreme that they name: Each row child_map[k] is injective. Say child index u lies in grid row (u // 64) mod 16 and grid column (u // 128) mod 8, and parent index v lies in row block v // 384 and column block v // 1536. Of one grid row's child indices at most 27 map into one row block, and this is reached in every draw; of one grid column's child indices exactly 144 map into each column block. Each children[k] is symmetric positive definite in logical order. Each pivot_inverse[k, p] is lower triangular.
All inputs are finite; a program needn't handle non-finite values.
Results may differ from a plain program's by a relative error of at most 0.0081.
Values may be sent and summed in bfloat16 or wider, within the bound.
A program may use at most 128 MiB of HBM per device.

v0:
```python
import jax
import jax.numpy as jnp
from jax import lax
from jax.sharding import PartitionSpec as P

P_SIZE = 1024
NPAN = 3


def spread(value, axis, source):
    kept = jnp.where(lax.axis_index(axis) == source, value, 0).astype(value.dtype)
    return lax.psum(kept, axis)


def subtract_product(matrix, row_start, col_start, left_rows, right_rows):
    update = lax.dot_general(
        left_rows, right_rows, (((1,), (1,)), ((), ())), preferred_element_type=jnp.float32
    )
    return matrix.at[row_start:, col_start:].add(-update)


def place_slots(destination, blocks, capacity):
    onehot = (destination[..., None] == jnp.arange(blocks, dtype=jnp.int32)).astype(jnp.int32)
    slot_rank = jnp.sum(jnp.cumsum(onehot, -2) * onehot, -1) - 1
    return destination * capacity + slot_rank


def device_order(values, groups, piece):
    child_span = values.shape[1]
    shaped = values.reshape(2, child_span // P_SIZE, groups, piece).transpose(0, 2, 1, 3)
    return shaped.reshape(2, groups, child_span // groups)


def on_device(children, pivot_inverse, parent_front, child_map):
    grid_rows = lax.axis_size("row")
    grid_cols = lax.axis_size("col")
    front_index = lax.axis_index("front")
    row_index = lax.axis_index("row")
    col_index = lax.axis_index("col")
    matrix = children[0]
    local_rows, local_cols = matrix.shape
    piece_rows = P_SIZE // grid_rows
    piece_cols = P_SIZE // grid_cols
    grid_ratio = grid_rows // grid_cols
    factor = jnp.zeros((local_rows, NPAN * piece_cols), jnp.bfloat16)
    deferred = None
    for panel_index in range(NPAN):
        row_top = panel_index * piece_rows
        col_left = panel_index * piece_cols
        row_next = row_top + piece_rows
        col_next = col_left + piece_cols
        column_piece = matrix[row_top:, col_left:col_next].astype(jnp.bfloat16)
        gathered = lax.all_gather(column_piece, "col", axis=1, tiled=True)
        inverse_whole = lax.all_gather(pivot_inverse[0, panel_index], "row", axis=0, tiled=True)
        left_all = lax.dot_general(
            gathered, inverse_whole, (((1,), (1,)), ((), ())), preferred_element_type=jnp.float32
        ).astype(jnp.bfloat16)
        left_rows = left_all[piece_rows:]
        factor = factor.at[row_top:, col_left:col_next].set(
            lax.dynamic_slice_in_dim(left_all, col_index * piece_cols, piece_cols, 1)
        )
        pieces = []
        for member in range(grid_ratio):
            pieces.append(spread(left_rows, "row", col_index * grid_ratio + member))
        blocks_left = left_rows.shape[0] // piece_rows
        shaped = [received.reshape(blocks_left, piece_rows, P_SIZE) for received in pieces]
        right_rows = jnp.stack(shaped, 1).reshape(blocks_left * piece_cols, P_SIZE)
        matrix = subtract_product(matrix, row_next, col_next, left_rows, right_rows)
    schur = matrix[NPAN * piece_rows :, NPAN * piece_cols :].astype(jnp.bfloat16)
    schur_rows, schur_cols = schur.shape
    parent_rows, parent_cols = parent_front.shape
    blocks = 2 * grid_rows
    row_capacity = 3 * schur_rows // (4 * grid_rows)
    col_capacity = schur_cols // grid_cols
    sent_total = blocks * row_capacity
    block_index = front_index * grid_rows + row_index
    row_parent = device_order(child_map, grid_rows, piece_rows)
    row_dest = row_parent // parent_rows
    row_slot = place_slots(row_dest, blocks, row_capacity)
    own_slots = lax.dynamic_index_in_dim(
        lax.dynamic_index_in_dim(row_slot, front_index, 0, keepdims=False),
        row_index,
        0,
        keepdims=False,
    )
    row_positions = jnp.arange(schur_rows, dtype=jnp.int32)
    row_source = jnp.zeros((sent_total,), jnp.int32).at[own_slots].set(row_positions)
    outgoing = schur[row_source].reshape(blocks, row_capacity, schur_cols)
    incoming = lax.all_to_all(outgoing, ("front", "row"), split_axis=0, concat_axis=0, tiled=True)
    source_device = (
        jnp.arange(2, dtype=jnp.int32)[:, None, None] * grid_rows
        + jnp.arange(grid_rows, dtype=jnp.int32)[None, :, None]
    )
    row_flat = source_device * row_capacity + row_slot - row_dest * row_capacity
    sibling_base = jnp.arange(2, dtype=jnp.int32)[:, None, None] * parent_rows
    row_target = jnp.where(
        row_dest == block_index,
        sibling_base + row_parent - block_index * parent_rows,
        2 * parent_rows,
    )
    row_lookup = (
        jnp.full((2 * parent_rows + 1,), sent_total, jnp.int32)
        .at[row_target.reshape(-1)]
        .set(row_flat.reshape(-1))[: 2 * parent_rows]
    )
    padded_rows = jnp.concatenate(
        [incoming.reshape(sent_total, schur_cols), jnp.zeros((1, schur_cols), jnp.bfloat16)], 0
    )
    assembled = padded_rows[row_lookup].reshape(2, parent_rows, schur_cols)
    col_parent = device_order(child_map, grid_cols, piece_cols)
    col_dest = col_parent // parent_cols
    col_slot = place_slots(col_dest, grid_cols, col_capacity)
    sent_cols = grid_cols * col_capacity
    sibling_rows = jnp.arange(2, dtype=jnp.int32)[:, None]
    own_cols = lax.dynamic_index_in_dim(col_slot, col_index, 1, keepdims=False)
    col_positions = jnp.arange(schur_cols, dtype=jnp.int32)
    col_source = (
        jnp.zeros((2, sent_cols), jnp.int32)
        .at[sibling_rows, own_cols]
        .set(jnp.broadcast_to(col_positions, (2, schur_cols)))
    )
    outgoing_cols = jnp.take_along_axis(assembled, col_source[:, None, :], axis=2).reshape(
        2, parent_rows, grid_cols, col_capacity
    )
    arrived = lax.all_to_all(outgoing_cols, "col", split_axis=2, concat_axis=2, tiled=True)
    col_flat = (
        jnp.arange(grid_cols, dtype=jnp.int32)[None, :, None] * col_capacity
        + col_slot
        - col_dest * col_capacity
    )
    col_target = jnp.where(col_dest == col_index, col_parent - col_index * parent_cols, parent_cols)
    sibling_grid = jnp.broadcast_to(jnp.arange(2, dtype=jnp.int32)[:, None, None], col_target.shape)
    col_lookup = (
        jnp.full((2, parent_cols + 1), sent_cols, jnp.int32)
        .at[sibling_grid.reshape(-1), col_target.reshape(-1)]
        .set(col_flat.reshape(-1))[:, :parent_cols]
    )
    padded_cols = jnp.concatenate(
        [arrived.reshape(2, parent_rows, sent_cols), jnp.zeros((2, parent_rows, 1), jnp.bfloat16)],
        2,
    )
    placed = jnp.take_along_axis(padded_cols, col_lookup[:, None, :], axis=2)
    parent_out = parent_front + placed[0].astype(jnp.float32) + placed[1].astype(jnp.float32)
    return (parent_out, factor[None])


def solution(mesh):
    in_specs = (
        P("front", "row", "col"),
        P("front", None, "row", None),
        P(("front", "row"), "col"),
        P(),
    )
    out_specs = (P(("front", "row"), "col"), P("front", "row", "col"))
    return jax.shard_map(
        on_device, mesh=mesh, in_specs=in_specs, out_specs=out_specs, check_vma=False
    )
```

profile of v0, /device:TPU:1, one launch (start us, length us, event | category | flops | bytes accessed | tf_op | source)
XLA Modules:
  0.0 887.5 jit_solution(6497201730904579678)
XLA Ops:
  7.2 2.7 convert_bitcast_fusion.1
  11.5 42.8 %all-gather.10.cloned.1.call-done = bf16[768,1024]{1,0:T(8,128)(2,1)} async-done(((bf16[768,128]{1,0:T(8,128)(2,1)}), bf16[768,1024]{1,0:T(8,128)(2,1)}) %all-gather.10.cloned.1.call-update) | async-done | bytes 1572880 | tf_op jit(solution)/shard_map/all_gather | solution.py:53
  54.3 54.8 %all-gather.16.cloned.1.call-done = bf16[1,1,1024,1024]{3,2,1,0:T(8,128)(2,1)} async-done(((bf16[1,1,64,1024]{3,2,1,0:T(8,128)(2,1)}), bf16[1,1,1024,1024]{3,2,1,0:T(8,128)(2,1)}) %all-gather.16.cloned.1.call-update) | async-done | bytes 2097168 | tf_op jit(solution)/shard_map/all_gather | solution.py:54
  109.2 3.9 fusion.10
  115.6 104.0 %all-reduce.15.cloned.1.call-done = (bf16[11,1,64,1024]{3,2,1,0:T(8,128)(2,1)}, bf16[11,1,64,1024]{3,2,1,0:T(8,128)(2,1)}) async-done(((bf16[11,1,64,1024]{3,2,1,0:T(8,128)(2,1)}, bf16[11,1,64,1024]{3,2,1,0:T(8,128)(2,1)}), (bf16[11,1,64,1024]{3,2,1,0:T(8,128)(2,1)}, bf16[11,1,64,1024]{3,2,1,0:T(8,128)(2,1)})) %all-reduce.15.cloned.1.call-update) | async-done | bytes 2883600 | tf_op jit(solution)/shard_map/psum | solution.py:12
  221.7 4.6 bitcast_add_fusion
  229.0 41.9 %all-gather.18.cloned.1.call-done = bf16[1,1,1024,1024]{3,2,1,0:T(8,128)(2,1)} async-done(((bf16[1,1,64,1024]{3,2,1,0:T(8,128)(2,1)}), bf16[1,1,1024,1024]{3,2,1,0:T(8,128)(2,1)}) %all-gather.18.cloned.1.call-update) | async-done | bytes 2097168 | tf_op jit(solution)/shard_map/all_gather | solution.py:54
  270.9 41.5 %all-gather.12.cloned.1.call-done = bf16[704,1024]{1,0:T(8,128)(2,1)} async-done(((bf16[704,128]{1,0:T(8,128)(2,1)}), bf16[704,1024]{1,0:T(8,128)(2,1)}) %all-gather.12.cloned.1.call-update) | async-done | bytes 1441808 | tf_op jit(solution)/shard_map/all_gather | solution.py:53
  312.4 3.7 fusion.13
  323.5 80.4 %reduce-window.16 = s32[2,16,32,5,128]{4,2,3,1,0:T(8,128)S(1)} reduce-window(s32[2,16,32,5,128]{4,2,3,1,0:T(8,128)} %copy_bitcast_fusion, s32[]{:T(128)} %constant.270.clone.1), window={size=1x1x1x1x128 pad=0_0x0_0x0_0x0_0x127_0}, to_apply=%region_11.12 | reduce-window | flops 83230720 | bytes 5242884 | tf_op jit(solution)/shard_map/reduce-window.2
  406.2 2.8 copy.44
  410.9 4.3 scatter_custom_fusion
  415.7 36.3 %reduce-window.14 = s32[2,8,8,9,128]{4,3,2,1,0:T(8,128)S(1)} reduce-window(s32[2,8,8,9,128]{4,3,2,1,0:T(8,128)S(1)} %fusion.20, s32[]{:T(128)} %constant.270.clone.1), window={size=1x1x1x1x128 pad=0_0x0_0x0_0x0_0x127_0}, to_apply=%region_0.0 | reduce-window | flops 18726912 | bytes 1179652 | tf_op jit(solution)/shard_map/reduce-window
  452.0 2.5 slice_reduce_fusion
  454.5 2.5 reduce-window.15
  462.5 3.8 fusion
  469.9 5.1 all-gather.20.cloned.1.call-done
  475.0 40.6 %all-gather.14.cloned.1.call-done = bf16[640,1024]{1,0:T(8,128)(2,1)} async-done(((bf16[640,128]{1,0:T(8,128)(2,1)}), bf16[640,1024]{1,0:T(8,128)(2,1)}) %all-gather.14.cloned.1.call-update) | async-done | bytes 1310736 | tf_op jit(solution)/shard_map/all_gather | solution.py:53
  515.6 3.5 fusion.16
  521.6 103.0 %all-reduce.11.cloned.1.call-done = (bf16[9,1,64,1024]{3,2,1,0:T(8,128)(2,1)}, bf16[9,1,64,1024]{3,2,1,0:T(8,128)(2,1)}) async-done(((bf16[9,1,64,1024]{3,2,1,0:T(8,128)(2,1)}, bf16[9,1,64,1024]{3,2,1,0:T(8,128)(2,1)}), (bf16[9,1,64,1024]{3,2,1,0:T(8,128)(2,1)}, bf16[9,1,64,1024]{3,2,1,0:T(8,128)(2,1)})) %all-reduce.11.cloned.1.call-update) | async-done | bytes 2359312 | tf_op jit(solution)/shard_map/psum | solution.py:12
  629.0 3.9 gather_fusion
  635.0 6.6 all-to-all-start
  644.2 9.0 %scatter_custom_fusion.3 = s32[2304]{0:T(1024)S(1)} fusion(s32[2304]{0:T(1024)S(1)} %reshape.780, s32[2304]{0:T(1024)S(1)} %reshape.782, s32[]{:T(128)} %constant.270.clone.1), kind=kCustom, calls=%fused_computation.121 | custom fusion | bytes 9220
  653.6 68.0 %scatter_custom_fusion.1 = s32[769]{0:T(1024)S(1)} fusion(s32[18432]{0:T(1024)} %bitcast.174, s32[18432]{0:T(1024)S(1)} %add_subtract_fusion, s32[]{:T(128)} %constant.290.clone.1), kind=kCustom, calls=%fused_computation.130 | custom fusion | bytes 3588 | tf_op jit(solution)/shard_map/scatter | solution.py:104
  725.5 3.6 gather_fusion.1
  729.1 2.8 copy.47
  731.9 19.8 %gather_fusion.2 = bf16[2304,384]{1,0:T(8,128)(2,1)} fusion(bf16[2,384,1152]{1,2,0:T(8,128)(2,1)S(1)} %copy.47, s32[2304]{0:T(1024)S(1)} %reshape.746), kind=kCustom, calls=%fused_computation.2 | custom fusion | bytes 3557376 | tf_op jit(solution)/shard_map/jit(take_along_axis)/gather | solution.py:122
  751.7 8.9 %broadcast_select_fusion = bf16[2,384,8,144]{1,0,3,2:T(2,128)(2,1)} fusion(pred[2,8,144]{0,2,1:T(8,128)(4,1)S(1)} %bitcast.171, bf16[2,384,8,144]{1,3,2,0:T(8,128)(2,1)} %bitcast.158), kind=kLoop, calls=%fused_computation.9 | loop fusion | flops 884736 | bytes 3541248 | tf_op jit(solution)/shard_map/jit(take_along_axis)/select_n | solution.py:122
  760.7 6.9 all-to-all-start.1
  768.4 67.8 %scatter_custom_fusion.2 = s32[3074]{0:T(1024)S(1)} fusion(s32[18432]{0:T(1024)S(1)} %broadcast_select_fusion.7, s32[18432]{0:T(1024)S(1)} %add_subtract_fusion.1, s32[]{:T(128)} %constant.269.clone.1), kind=kCustom, calls=%fused_computation.119 | custom fusion | bytes 12300
  843.5 31.1 %gather_fusion.3 = bf16[3072,384]{1,0:T(8,128)(2,1)} fusion(bf16[2,384,1153]{1,0,2:T(2,128)(2,1)S(1)} %concatenate.27, s32[3072]{0:T(1024)S(1)} %reshape.752), kind=kCustom, calls=%fused_computation.3 | custom fusion | bytes 4743168 | tf_op jit(solution)/shard_map/jit(take_along_axis)/gather | solution.py:142
  874.5 2.8 copy.49
  (187 shorter events, 56.6 us)
Async XLA Ops:
  7.2 3.5 copy-start.11
  7.2 47.2 %all-gather.10.cloned.1.call-start = ((), (), s32[]{:S(2)}) async-start(), calls=%async_computation.2 | async-start | bytes 1769472 | tf_op jit(solution)/shard_map/all_gather | solution.py:53
  10.6 98.6 %all-gather.16.cloned.1.call-start = ((), (), s32[]{:S(2)}) async-start(), calls=%async_computation.5 | async-start | bytes 2228224 | tf_op jit(solution)/shard_map/all_gather | solution.py:54
  11.4 208.2 %all-reduce.15.cloned.1.call-start = ((), (), s32[]{:S(2)}) async-start(), calls=%async_computation.10 | async-start | bytes 5767168 | tf_op jit(solution)/shard_map/psum | solution.py:12
  113.1 108.6 %copy-start.3 = (bf16[768,1024]{1,0:T(8,128)(2,1)}, bf16[768,1024]{1,0:T(8,128)(2,1)S(1)}, u32[]{:S(2)}) copy-start(bf16[768,1024]{1,0:T(8,128)(2,1)S(1)} %fusion.10) | copy-start | bytes 4718596
  115.0 155.9 %all-gather.18.cloned.1.call-start = ((), (), s32[]{:S(2)}) async-start(), calls=%async_computation.6 | async-start | bytes 2228224 | tf_op jit(solution)/shard_map/all_gather | solution.py:54
  115.6 196.8 %all-gather.12.cloned.1.call-start = ((), (), s32[]{:S(2)}) async-start(), calls=%async_computation.3 | async-start | bytes 1622016 | tf_op jit(solution)/shard_map/all_gather | solution.py:53
  228.9 231.2 %all-reduce.13.cloned.1.call-start = ((), (), s32[]{:S(2)}) async-start(), calls=%async_computation.9 | async-start | bytes 5242880 | tf_op jit(solution)/shard_map/psum | solution.py:12
  316.1 1.9 copy-start.4
  318.1 156.9 %all-gather.20.cloned.1.call-start = ((), (), s32[]{:S(2)}) async-start(), calls=%async_computation.7 | async-start | bytes 2228224 | tf_op jit(solution)/shard_map/all_gather | solution.py:54
  318.8 196.8 %all-gather.14.cloned.1.call-start = ((), (), s32[]{:S(2)}) async-start(), calls=%async_computation.4 | async-start | bytes 1474560 | tf_op jit(solution)/shard_map/all_gather | solution.py:53
  319.2 2.4 copy-start.1
  410.8 41.1 %copy-start.12 = (s32[2,16,576]{2,1,0:T(8,128)}, s32[2,16,576]{2,1,0:T(8,128)S(1)}, u32[]{:S(2)}) copy-start(s32[2,16,576]{2,1,0:T(8,128)S(1)} %broadcast_add_fusion.1) | copy-start | bytes 221188
  457.8 4.6 copy-start.14
  460.1 2.3 copy-start.5
  468.7 155.9 %all-reduce.11.cloned.1.call-start = ((), (), s32[]{:S(2)}) async-start(), calls=%async_computation.8 | async-start | bytes 4718592 | tf_op jit(solution)/shard_map/psum | solution.py:12
  519.1 107.5 %copy-start.6 = (bf16[640,1024]{1,0:T(8,128)(2,1)}, bf16[640,1024]{1,0:T(8,128)(2,1)S(1)}, u32[]{:S(2)}) copy-start(bf16[640,1024]{1,0:T(8,128)(2,1)S(1)} %fusion.16) | copy-start | bytes 3932164
  624.6 2.6 copy-start.25
  635.0 6.7 copy-start.13
  635.0 6.8 copy-start.2
  635.0 7.0 copy-start.15
  635.0 9.1 %copy-start.21 = (s32[2,1152]{1,0:T(2,128)S(1)}, s32[2,1152]{1,0:T(2,128)}, u32[]{:S(2)}) copy-start(s32[2,1152]{1,0:T(2,128)} %broadcast_select_fusion.8) | copy-start | bytes 27652
  635.0 86.6 %all-to-all-start = ((bf16[32,27,1152]{2,1,0:T(8,128)(2,1)}), bf16[32,27,1152]{2,1,0:T(8,128)(2,1)S(1)}, u32[]{:S(2)}, u32[]{:S(2)}) async-start(bf16[32,27,1152]{2,1,0:T(8,128)(2,1)} %reshape.711), calls=%async_computation | async-start | bytes 4718592 | tf_op jit(solution)/shard_map/all_to_all | solution.py:89
  760.6 7.0 copy-start.8
  760.7 7.0 copy-start.9
  760.7 7.0 copy-start.27
  760.7 7.3 copy-start.26
  760.7 7.7 copy-start.16
  760.7 7.7 copy-start.17
  760.7 7.7 copy-start.20
  760.7 80.5 %all-to-all-start.1 = ((bf16[2,384,8,144]{1,0,3,2:T(2,128)(2,1)}), bf16[2,384,8,144]{1,0,3,2:T(2,128)(2,1)S(1)}, u32[]{:S(2)}, u32[]{:S(2)}) async-start(bf16[2,384,8,144]{1,0,3,2:T(2,128)(2,1)} %broadcast_select_fusion), calls=%async_computation.1 | async-start | bytes 3538944 | tf_op jit(solution)/shard_map/all_to_all | solution.py:125
  874.5 2.9 copy-start.22
  (9 other events, 10.3 us)
Sparse Core Ops, SparseCore 0:
  10.7 43.5 all-gather.9
  57.3 51.7 all-gather.15
  115.1 104.4 all-reduce.14
  222.2 48.6 all-gather.17
  273.1 39.1 all-gather.11
  318.2 105.2 all-reduce.12
  425.9 48.9 all-gather.19
  477.3 38.2 all-gather.13
  521.0 103.5 all-reduce.10
where the time goes:
time: 894 us; the launch traced here: 887 us
  waiting for transfers between devices  435 us (49%)
  local copies, waits for them, and re-layouts  244 us (27%)
  other arithmetic  158 us (18%)
  matrix products  21.3 us (2%)
  between operations  14.8 us (2%)
  starting transfers between devices  13.8 us (2%)
    psum x3, waiting for transfers between devices, spread(): return lax.psum(kept, axis)  207 us
    all_gather x3, waiting for transfers between devices, on_device(): gathered = lax.all_gather(column_piece, 'col', axis=1, tiled=True)  125 us
    another operation x9, other arithmetic  125 us
    all_gather x3, waiting for transfers between devices, on_device(): lax.all_gather(pivot_inverse[0, panel_index], 'row', axis=0, tiled=True)  102 us
    unnamed x63, local copies, waits for them, and re-layouts  83.7 us
    scatter x1, local copies, waits for them, and re-layouts, on_device(): row_lookup = jnp.full((2 * parent_rows + 1,), sent_total, jnp.int32).at[r...  68 us
    gather x3, local copies, waits for them, and re-layouts, on_device(): placed = jnp.take_along_axis(padded_cols, col_lookup[:, None, :], axis=2)  33.9 us
    gather x2, local copies, waits for them, and re-layouts, on_device(): jnp.take_along_axis(assembled, col_source[:, None, :], axis=2)  19.8 us
  transfers between devices with their start and end apart: 11, of which 8 were waited for; matrix products, arithmetic and copies ran while one was open for 35% of the time, Pallas kernels for 0%

commit v1 on v0

v1 whole, which is shorter than its diff:
```python
import functools

import jax
import jax.numpy as jnp
from jax import lax
from jax.experimental import pallas as pl
from jax.experimental.pallas import tpu as pltpu
from jax.sharding import PartitionSpec as P

MESH = pl.DeviceIdType.MESH
BF = jnp.bfloat16
F32 = jnp.float32
NPAN = 3
PANEL = 1024
LOCAL_ROWS, LOCAL_COLS = 768, 1536
ROW_PIECE, COL_PIECE = 64, 128
SCHUR_ROWS, SCHUR_COLS = 576, 1152
OUT_ROWS, OUT_COLS = 384, 1536
ROW_SLOT = 32
COL_SLOT = 144
PARTS = (48, 48, 32, 16)
PART_AT = (0, 48, 96, 128)
INV_COLS = 640
N_SEMS = 450
NT = (((1,), (1,)), ((), ()))


def dot(a, b):
    return jnp.dot(a, b, preferred_element_type=F32)


def dot_nt(a, b):
    return lax.dot_general(a, b, NT, preferred_element_type=F32)


class Net:
    def __init__(self, send_sems, recv_sems):
        self.send_sems, self.recv_sems = send_sems, recv_sems
        self.count, self.pending = 0, []

    def copy(self, index, src, dst, device):
        return pltpu.make_async_remote_copy(
            src_ref=src,
            dst_ref=dst,
            send_sem=self.send_sems.at[index],
            recv_sem=self.recv_sems.at[index],
            device_id=device,
            device_id_type=MESH,
        )

    def send(self, src, dst, device):
        index = self.count
        self.count += 1
        copy = self.copy(index, src, dst, device)
        copy.start()
        self.pending.append(copy)
        return index

    def recv(self, index, region, device):
        self.copy(index, region, region, device).wait_recv()

    def drain(self):
        for copy in self.pending:
            copy.wait_send()
        self.pending = []


def ring4(net, region, me, device, then):
    up, down, far = lax.rem(me + 1, 4), lax.rem(me + 3, 4), lax.rem(me + 2, 4)
    ids = {}
    ids["a"] = net.send(region(me, None), region(me, None), device(up))
    ids["b"] = net.send(region(me, None), region(me, None), device(down))

    def from_down():
        net.recv(ids["a"], region(down, None), device(up))
        ids["c"] = net.send(region(down, 0), region(down, 0), device(up))
        then(1, down)

    def from_up():
        net.recv(ids["b"], region(up, None), device(down))
        ids["d"] = net.send(region(up, 1), region(up, 1), device(down))
        then(2, up)

    def far_first():
        net.recv(ids["c"], region(far, 0), device(up))

    def far_second():
        net.recv(ids["d"], region(far, 1), device(down))
        then(3, far)

    return [from_down, from_up, far_first, far_second]


GRID_ORDER = (
    ("A", 1, 0), ("A", 1, 1), ("A", 1, 2), ("A", 1, 3), ("a", 0, 0), ("a", 0, 1), ("a", 1, 0),
    ("a", 1, 1), ("a", 2, 0), ("a", 2, 1), ("a", 3, 0), ("a", 3, 1), ("a", 0, 2), ("a", 0, 3),
    ("a", 1, 2), ("a", 1, 3), ("a", 2, 2), ("a", 2, 3), ("a", 3, 2), ("a", 3, 3),
)


def gather_grid(net, region, x, y):
    along_x = lambda v: {"row": y * 4 + v}
    along_y = lambda v: {"row": v * 4 + x}
    second = {("a", k): [] for k in range(4)} | {("b", k): [] for k in range(4)}
    done = lambda k, v: None

    def start_a(k, xx):
        second["a", k] += ring4(net, lambda v, part: region(v * 4 + xx, 0, part), y, along_y, done)

    def start_b(k, yy):
        second["b", k] += ring4(net, lambda v, part: region(yy * 4 + v, 1, part), x, along_x, done)

    first_a = ring4(net, lambda v, part: region(y * 4 + v, 0, part), x, along_x, start_a)
    first_b = ring4(net, lambda v, part: region(v * 4 + x, 1, part), y, along_y, start_b)
    start_a(0, x)
    start_b(0, y)

    def event(group, k, step):
        if group == "A":
            first_a[step]()
        elif group == "B":
            first_b[step]()
        else:
            second[group, k][step]()

    order = [(g, k, step) for way, k, step in GRID_ORDER for g in (way, chr(ord(way) + 1))]
    return [functools.partial(event, *item) for item in order]


def gather_ring8(net, region, me):
    ways = ({"col": lax.rem(me + 1, 8)}, {"col": lax.rem(me + 7, 8)})
    sign = (-1, 1)
    ids = {}
    for way in (0, 1):
        for half in (way, 1 - way):
            ids[way, 0, half] = net.send(region(me, half), region(me, half), ways[way])

    def event(way, step, half):
        block = lax.rem(me + 8 + sign[way] * step, 8)
        net.recv(ids[way, step - 1, half], region(block, half), ways[way])
        if step < 3 or (step == 3 and half == way):
            ids[way, step, half] = net.send(region(block, half), region(block, half), ways[way])

    order = []
    for step in (1, 2, 3):
        for j in (0, 1):
            order += [(0, step, j), (1, step, 1 - j)]
    order += [(0, 4, 0), (1, 4, 1)]
    return [functools.partial(event, *item) for item in order]


def merge(*lists):
    keyed = []
    for which, items in enumerate(lists):
        for i, item in enumerate(items):
            keyed.append(((i + 0.5) / len(items), which, i, item))
    return [item for *_, item in sorted(keyed, key=lambda k: k[:3])]


def run(items):
    for item in items:
        item()


def iota(shape, dim):
    return lax.broadcasted_iota(jnp.int32, shape, dim)


def kernel(
    children, inverse, parent, child_map,
    out, factor,
    a, wr, wc, inv, lr, lc,
    select_cols, select_rows, place_rows, place_cols,
    loan, schur, s1, g, o2, h,
    maps_in, row_parent, col_parent, slot_c, slot_r, rank_r, rank_c, want_r, want_c,
    local_sems, pre_send, pre_recv, send_sems, recv_sems,
):
    front, row, col = lax.axis_index("front"), lax.axis_index("row"), lax.axis_index("col")
    x, y = lax.rem(row, 4), row // 4
    block = front * 16 + row

    def load(i, src, dst):
        copy = pltpu.make_async_copy(src, dst, local_sems.at[i])
        copy.start()
        return copy

    own_rows = lambda ref, b, n: ref.at[pl.ds(pl.multiple_of(b * n, n), n)]
    load_left = load(0, children.at[0, :, pl.ds(0, 128)], a.at[:, pl.ds(0, 128)])
    load_top = load(
        1, children.at[0, pl.ds(0, 64), pl.ds(128, 1408)], a.at[pl.ds(0, 64), pl.ds(128, 1408)]
    )
    load_inv = [
        load(2 + p, inverse.at[0, p], inv.at[p, pl.ds(pl.multiple_of(row * 64, 64), 64)])
        for p in range(NPAN)
    ]

    barrier = pltpu.get_barrier_semaphore()
    for k in range(1, 8):
        pl.semaphore_signal(
            barrier, inc=1, device_id={"col": lax.rem(col + k, 8)}, device_id_type=MESH
        )
    for k in range(1, 32):
        other = lax.rem(block + k, 32)
        pl.semaphore_signal(
            barrier,
            inc=1,
            device_id={"front": other // 16, "row": lax.rem(other, 16)},
            device_id_type=MESH,
        )

    load_rest = load(
        5, children.at[0, pl.ds(64, 704), pl.ds(128, 1408)], a.at[pl.ds(64, 704), pl.ds(128, 1408)]
    )
    load_parent = load(6, parent, out)
    load_maps = load(7, child_map, maps_in)

    net = Net(send_sems, recv_sems)
    lane_c = pl.ds(pl.multiple_of(col * 128, 128), 128)
    rows_r = pl.ds(pl.multiple_of(row * 64, 64), 64)

    def in_block(b, half, part):
        if part is None:
            return pl.ds(pl.multiple_of(b * 64 + half * 32, 32), 32)
        return pl.ds(pl.multiple_of(b * 64 + half * 32 + part * 16, 16), 16)

    def start_ring(p):
        top = p * ROW_PIECE
        half_rows = (LOCAL_ROWS - top) // 2

        def region(b, half):
            return wr.at[
                p,
                pl.ds(top + half * half_rows, half_rows),
                pl.ds(pl.multiple_of(b * 128, 128), 128),
            ]

        return gather_ring8(net, region, col)

    def start_grid(p):
        left = (p + 1) * COL_PIECE

        def region(b, half, part):
            return wc.at[p, in_block(b, half, part), pl.ds(left, LOCAL_COLS - left)]

        return gather_grid(net, region, x, y)

    def lend(p, width):
        to = {"row": (3 - y) * 4 + x}
        return pltpu.make_async_remote_copy(
            src_ref=inv.at[p, rows_r, pl.ds(640, width)],
            dst_ref=loan.at[p, :, pl.ds(0, width)],
            send_sem=pre_send.at[p],
            recv_sem=pre_recv.at[p],
            device_id=to,
            device_id_type=MESH,
        )

    def lend_inverses():
        for p in range(NPAN):
            load_inv[p].wait()

        @pl.when(y == 3)
        def _():
            for p in range(NPAN):
                lend(p, 384).start()

        @pl.when(y == 2)
        def _():
            for p in range(NPAN):
                lend(p, 128).start()

    def start_inverse(p):
        @pl.when(y == 0)
        def _():
            lend(p, 384).wait_recv()
            inv[p, rows_r, 256:640] = loan[p, :, 0:384]

        @pl.when(y == 1)
        def _():
            lend(p, 128).wait_recv()
            inv[p, rows_r, 512:640] = loan[p, :, 0:128]

        def region(b, half, part):
            return inv.at[p, in_block(b, half, part), pl.ds(0, INV_COLS)]

        return gather_grid(net, region, x, y)

    def unfold_inverse(p):
        @pl.when(y == 3)
        def _():
            lend(p, 384).wait_send()

        @pl.when(y == 2)
        def _():
            lend(p, 128).wait_send()

        inv[p, 768:1024, 640:1024] = inv[p, 0:256, 256:640]
        inv[p, 512:768, 640:768] = inv[p, 256:512, 512:640]

    load_left.wait()
    wr[0, :, lane_c] = a[:, 0:128].astype(BF)
    load_top.wait()
    wc[0, rows_r, 128:] = a[0:64, 128:].astype(BF)
    pl.semaphore_wait(barrier, 38)
    ring = start_ring(0)
    grid = start_grid(0)
    lend_inverses()
    inverse_events = start_inverse(0)

    tri = select_cols

    def build_tri(i, carry):
        r0 = pl.multiple_of(i * 128, 128)
        below = iota((128, SCHUR_COLS), 0) + r0 < iota((128, SCHUR_COLS), 1)
        tri[pl.ds(r0, 128), :] = below.astype(F32).astype(BF)
        return carry

    def group_maps():
        load_maps.wait()
        for child in range(2):
            for t in range(9):
                for b in range(16):
                    start = t * PANEL + b * ROW_PIECE
                    row_parent[
                        child * 16 + b : child * 16 + b + 1, t * ROW_PIECE : (t + 1) * ROW_PIECE
                    ] = maps_in[child : child + 1, start : start + ROW_PIECE]
                for b in range(8):
                    start = t * PANEL + b * COL_PIECE
                    col_parent[
                        child * 8 + b : child * 8 + b + 1, t * COL_PIECE : (t + 1) * COL_PIECE
                    ] = maps_in[child : child + 1, start : start + COL_PIECE]

    def make_tri():
        lax.fori_loop(0, SCHUR_COLS // 128, build_tri, 0)

    def as_f(mask):
        return jnp.where(mask, 1.0, 0.0).astype(F32)

    def send_slots_cols():
        mine = col_parent[pl.ds(front * 8 + col, 1), :]
        low = iota((8, SCHUR_COLS), 0) * OUT_COLS
        hot = as_f((mine >= low) & (mine < low + OUT_COLS))
        before = dot(hot.astype(BF), tri[...])
        rank = jnp.sum(hot * before, 0, keepdims=True)
        dest = jnp.sum(hot * iota((8, SCHUR_COLS), 0).astype(F32), 0, keepdims=True)
        part_at, size = PART_AT[0], PARTS[0]
        for j in range(1, len(PARTS)):
            later = as_f(rank >= PART_AT[j])
            part_at = part_at + later * (PART_AT[j] - PART_AT[j - 1])
            size = size + later * (PARTS[j] - PARTS[j - 1])
        slot = rank + 7.0 * part_at + dest * size
        slot_c[...] = jnp.broadcast_to(slot, (8, SCHUR_COLS))

    def send_slots_rows():
        mine = row_parent[pl.ds(front * 16 + row, 1), :]
        low = iota((32, SCHUR_ROWS), 0) * OUT_ROWS
        hot = as_f((mine >= low) & (mine < low + OUT_ROWS))
        before = dot(hot.astype(BF), tri[0:SCHUR_ROWS, 0:SCHUR_ROWS])
        rank = jnp.sum(hot * before, 0, keepdims=True)
        dest = jnp.sum(hot * iota((32, SCHUR_ROWS), 0).astype(F32), 0, keepdims=True)
        slot_r[...] = jnp.broadcast_to(dest * ROW_SLOT + rank, (8, SCHUR_ROWS))

    def receive_ranks():
        low = block * OUT_ROWS
        there = row_parent[...]
        here = as_f((there >= low) & (there < low + OUT_ROWS))
        before = dot(here.astype(BF), tri[0:SCHUR_ROWS, 0:SCHUR_ROWS])
        rank_r[...] = jnp.where(here > 0.5, before, -1.0)
        low_c = col * OUT_COLS
        there = col_parent[...]
        here = as_f((there >= low_c) & (there < low_c + OUT_COLS))
        before = dot(here.astype(BF), tri[...])
        rank_c[...] = jnp.where(here > 0.5, before, -1.0)

    def wanted_rows(i, carry):
        rank = rank_r[pl.ds(i, 1), :]
        value = (row_parent[pl.ds(i, 1), :] - block * OUT_ROWS + 1).astype(F32)
        match = rank == iota((ROW_SLOT, SCHUR_ROWS), 0).astype(F32)
        want = jnp.sum(jnp.where(match, value, 0.0), 1, keepdims=True) - 1.0
        want_r[pl.ds(pl.multiple_of(i * ROW_SLOT, ROW_SLOT), ROW_SLOT), :] = jnp.broadcast_to(
            want, (ROW_SLOT, 128)
        )
        return carry

    def wanted_cols(i, carry):
        rank = rank_c[pl.ds(i, 1), :]
        value = (col_parent[pl.ds(i, 1), :] - col * OUT_COLS + 1).astype(F32)
        match = rank == iota((COL_SLOT, SCHUR_COLS), 0).astype(F32)
        want = jnp.sum(jnp.where(match, value, 0.0), 1, keepdims=True) - 1.0
        child, source = i // 8, lax.rem(i, 8)
        for size, start in zip(PARTS, PART_AT):
            at = child * SCHUR_COLS + 8 * start + source * size
            want_c[pl.ds(pl.multiple_of(at, 16), size), :] = jnp.broadcast_to(
                want[start : start + size], (size, 128)
            )
        return carry

    def make_wanted_rows():
        lax.fori_loop(0, 32, wanted_rows, 0)

    def make_wanted_cols():
        lax.fori_loop(0, 16, wanted_cols, 0)

    def build_select_cols(i, carry):
        r0 = pl.multiple_of(i * 128, 128)
        hit = slot_c[0:1, :] == (iota((128, SCHUR_COLS), 0) + r0).astype(F32)
        select_cols[pl.ds(r0, 128), :] = as_f(hit).astype(BF)
        return carry

    def build_select_rows(i, carry):
        r0 = pl.multiple_of(i * 128, 128)
        hit = slot_r[0:1, :] == (iota((128, SCHUR_ROWS), 0) + r0).astype(F32)
        select_rows[pl.ds(r0, 128), :] = as_f(hit).astype(BF)
        return carry

    def build_place_rows(i, carry):
        r0 = pl.multiple_of(i * 128, 128)
        hit = want_r[pl.ds(r0, 128), 0:1] == iota((128, OUT_ROWS), 1).astype(F32)
        child, at = i // 4, pl.multiple_of(lax.rem(i, 4) * 128, 128)
        place_rows[child, :, pl.ds(at, 128)] = as_f(hit).T.astype(BF)
        return carry

    def build_place_cols(i, carry):
        r0 = pl.multiple_of(i * 128, 128)
        hit = want_c[pl.ds(r0, 128), 0:1] == iota((128, OUT_COLS), 1).astype(F32)
        place_cols[pl.ds(r0, 128), :] = as_f(hit).astype(BF)
        return carry

    def make_selects():
        lax.fori_loop(0, SCHUR_COLS // 128, build_select_cols, 0)
        lax.fori_loop(0, 8, build_select_rows, 0)

    def make_place_rows():
        lax.fori_loop(0, 8, build_place_rows, 0)

    def make_place_cols(part):
        lax.fori_loop(part * 6, part * 6 + 6, build_place_cols, 0)

    maps = [
        group_maps, make_tri, send_slots_cols, send_slots_rows, receive_ranks, make_wanted_rows,
        make_wanted_cols, make_selects, make_place_rows,
    ] + [functools.partial(make_place_cols, part) for part in range(3)]

    def left_rows(p, i):
        top = p * ROW_PIECE
        tile, depth = pl.ds(i * 256, 256), pl.ds(0, (i + 1) * 256)
        lr[top:, tile] = dot_nt(wr[p, top:, depth], inv[p, tile, depth]).astype(BF)

    def left_cols(p, i):
        left = (p + 1) * COL_PIECE
        tile, depth = pl.ds(i * 256, 256), pl.ds(0, (i + 1) * 256)
        lc[tile, left:] = dot(inv[p, tile, depth], wc[p, depth, left:]).astype(BF)

    def left_work(p):
        return [functools.partial(f, p, i) for f in (left_rows, left_cols) for i in range(4)]

    def keep_factor(p):
        top = p * ROW_PIECE
        at = slice(p * COL_PIECE, (p + 1) * COL_PIECE)
        factor[top:, at] = lr[top:, lane_c]
        if p:
            factor[:top, at] = jnp.zeros((top, COL_PIECE), BF)

    def next_column(q):
        top, left = q * ROW_PIECE, q * COL_PIECE
        right = left + COL_PIECE
        piece = a[top:, left:right] - dot(lr[top:, :], lc[:, left:right])
        wr[q, top:, lane_c] = piece.astype(BF)

    def next_row(q):
        top, right = q * ROW_PIECE, (q + 1) * COL_PIECE
        piece = a[top : top + ROW_PIECE, right:] - dot(lr[top : top + ROW_PIECE, :], lc[:, right:])
        wc[q, rows_r, right:] = piece.astype(BF)

    def trailing(q, start, stop):
        top = (q + 1) * ROW_PIECE
        a[top:, start:stop] = a[top:, start:stop] - dot(lr[top:, :], lc[:, start:stop])

    def trailing_work(q):
        left = (q + 1) * COL_PIECE
        edges = list(range(left, LOCAL_COLS, 256)) + [LOCAL_COLS]
        return [functools.partial(trailing, q, s, e) for s, e in zip(edges, edges[1:])]

    run(merge(ring, grid, inverse_events, maps))
    load_rest.wait()
    for p in range(NPAN - 1):
        inverse_events = start_inverse(p + 1)
        unfold_inverse(p)
        work = left_work(p)
        run(work)
        next_column(p + 1)
        ring = start_ring(p + 1)
        next_row(p + 1)
        grid = start_grid(p + 1)
        rest = [functools.partial(keep_factor, p)] + trailing_work(p + 1)
        run(merge(ring, grid, inverse_events, rest))
    last = NPAN - 1
    unfold_inverse(last)
    run(left_work(last))
    for start in range(0, SCHUR_COLS, 384):
        at = slice(start, start + 384)
        cols = slice(NPAN * COL_PIECE + start, NPAN * COL_PIECE + start + 384)
        top = NPAN * ROW_PIECE
        schur[:, at] = (a[top:, cols] - dot(lr[top:, :], lc[:, cols])).astype(BF)

    def part_rows(j, b):
        return pl.ds(pl.multiple_of(8 * PART_AT[j] + b * PARTS[j], 16), PARTS[j])

    spans = [pl.ds(8 * start, 8 * size) for start, size in zip(PART_AT, PARTS)]
    sent_z = []
    for j, span in enumerate(spans):
        s1[span, :] = dot_nt(select_cols[span, :], schur[...]).astype(BF)
        ids = []
        for k in (1, 7, 2, 6, 3, 5, 4):
            to = lax.rem(col + k, 8)
            src, dst = s1.at[part_rows(j, to)], g.at[part_rows(j, col)]
            ids.append((k, net.send(src, dst, {"col": to})))
        g[part_rows(j, col), :] = s1[part_rows(j, col), :]
        sent_z.append(ids)
    keep_factor(last)
    sent_xy = []
    at_row = lambda b: pl.ds(pl.multiple_of(b * ROW_SLOT, ROW_SLOT), ROW_SLOT)
    for j, span in enumerate(spans):
        for k, index in sent_z[j]:
            source = lax.rem(col + 8 - k, 8)
            net.recv(index, g.at[part_rows(j, source)], {"col": source})
        o2[:, span] = dot_nt(select_rows[...], g[span, :]).astype(BF)
        ids = []
        for k in range(1, 32):
            to = lax.rem(block + k, 32)
            device = {"front": to // 16, "row": lax.rem(to, 16)}
            ids.append((k, net.send(o2.at[at_row(to), span], h.at[at_row(block), span], device)))
        h[at_row(block), span] = o2[at_row(block), span]
        sent_xy.append(ids)
    load_parent.wait()
    for j, span in enumerate(spans):
        for k, index in sent_xy[j]:
            source = lax.rem(block + 32 - k, 32)
            device = {"front": source // 16, "row": lax.rem(source, 16)}
            net.recv(index, h.at[at_row(source), span], device)
        for child in range(2):
            rows = dot(place_rows[child], h[pl.ds(child * 512, 512), span]).astype(BF)
            cols = place_cols[pl.ds(child * SCHUR_COLS + 8 * PART_AT[j], 8 * PARTS[j]), :]
            out[...] = out[...] + dot(rows, cols)
    net.drain()


def on_device(children, pivot_inverse, parent_front, child_map):
    vmem = pl.BlockSpec(memory_space=pltpu.VMEM)
    hbm = pl.BlockSpec(memory_space=pl.ANY)
    parent_out, factor = pl.pallas_call(
        kernel,
        out_shape=(
            jax.ShapeDtypeStruct((OUT_ROWS, OUT_COLS), F32),
            jax.ShapeDtypeStruct((LOCAL_ROWS, NPAN * COL_PIECE), BF),
        ),
        in_specs=[hbm, hbm, hbm, hbm],
        out_specs=(vmem, vmem),
        scratch_shapes=[
            pltpu.VMEM((LOCAL_ROWS, LOCAL_COLS), F32),
            pltpu.VMEM((NPAN, LOCAL_ROWS, PANEL), BF),
            pltpu.VMEM((NPAN, PANEL, LOCAL_COLS), BF),
            pltpu.VMEM((NPAN, PANEL, PANEL), BF),
            pltpu.VMEM((LOCAL_ROWS, PANEL), BF),
            pltpu.VMEM((PANEL, LOCAL_COLS), BF),
            pltpu.VMEM((SCHUR_COLS, SCHUR_COLS), BF),
            pltpu.VMEM((32 * ROW_SLOT, SCHUR_ROWS), BF),
            pltpu.VMEM((2, OUT_ROWS, 16 * ROW_SLOT), BF),
            pltpu.VMEM((2 * SCHUR_COLS, OUT_COLS), BF),
            pltpu.VMEM((NPAN, ROW_PIECE, 384), BF),
            pltpu.VMEM((SCHUR_ROWS, SCHUR_COLS), BF),
            pltpu.VMEM((SCHUR_COLS, SCHUR_ROWS), BF),
            pltpu.VMEM((SCHUR_COLS, SCHUR_ROWS), BF),
            pltpu.VMEM((32 * ROW_SLOT, SCHUR_COLS), BF),
            pltpu.VMEM((32 * ROW_SLOT, SCHUR_COLS), BF),
            pltpu.VMEM((2, 9216), jnp.int32),
            pltpu.VMEM((32, SCHUR_ROWS), jnp.int32),
            pltpu.VMEM((16, SCHUR_COLS), jnp.int32),
            pltpu.VMEM((8, SCHUR_COLS), F32),
            pltpu.VMEM((8, SCHUR_ROWS), F32),
            pltpu.VMEM((32, SCHUR_ROWS), F32),
            pltpu.VMEM((16, SCHUR_COLS), F32),
            pltpu.VMEM((32 * ROW_SLOT, 128), F32),
            pltpu.VMEM((2 * SCHUR_COLS, 128), F32),
            pltpu.SemaphoreType.DMA((8,)),
            pltpu.SemaphoreType.DMA((NPAN,)),
            pltpu.SemaphoreType.DMA((NPAN,)),
            pltpu.SemaphoreType.DMA((N_SEMS,)),
            pltpu.SemaphoreType.DMA((N_SEMS,)),
        ],
        compiler_params=pltpu.CompilerParams(
            collective_id=0, has_side_effects=True, vmem_limit_bytes=62 * 2**20
        ),
    )(
        children,
        pivot_inverse,
        parent_front,
        child_map,
    )
    return parent_out, factor[None]


def solution(mesh):
    in_specs = (
        P("front", "row", "col"),
        P("front", None, "row", None),
        P(("front", "row"), "col"),
        P(),
    )
    out_specs = (P(("front", "row"), "col"), P("front", "row", "col"))
    return jax.shard_map(
        on_device, mesh=mesh, in_specs=in_specs, out_specs=out_specs, check_vma=False
    )
```

time: 894 us -> 153 us (0.17)
  waiting for transfers between devices: 435 us -> 0 us
  local copies, waits for them, and re-layouts: 244 us -> 4.1 us
  other arithmetic: 158 us -> 0 us
  Pallas kernels: 0 us -> 148 us
  matrix products: 21.3 us -> 0 us
  between operations: 14.8 us -> 0.65 us
  starting transfers between devices: 13.8 us -> 0 us
    all_gather x6 -> x0, waiting for transfers between devices: 227 us -> none  [the longest x3 125 us: on_device(): gathered = lax.all_gather(column_piece, 'col', axis=1, tiled=True)]
    psum x3 -> x0, waiting for transfers between devices: 207 us -> none  [spread(): return lax.psum(kept, axis)]
    pallas_call x0 -> x1, Pallas kernels: none -> 148 us  [on_device(): pl.pallas_call(kernel, out_shape=(jax.ShapeDtypeStruct((OUT_ROWS, OUT_COL...]
    another operation x12 -> x0, other arithmetic: 131 us -> none
    unnamed x63 -> x4, local copies, waits for them, and re-layouts: 83.7 us -> 4.1 us
    scatter x6 -> x0, local copies, waits for them, and re-layouts: 74.3 us -> none  [the longest x1 68 us: on_device(): row_lookup = jnp.full((2 * parent_rows + 1,), sent_total, jnp.int32).at[r...]
    gather x7 -> x0, local copies, waits for them, and re-layouts: 61.3 us -> none  [the longest x3 33.9 us: on_device(): placed = jnp.take_along_axis(padded_cols, col_lookup[:, None, :], axis=2)]
    dot_general x6 -> x0, matrix products: 21.3 us -> none  [the longest x3 11.2 us: on_device(): lax.dot_general(gathered, inverse_whole, (((1,), (1,)), ((), ())), prefer...]
  transfers between devices with their start and end apart: 11 -> 0, of which waited for: 8 -> 0; matrix products, arithmetic and copies ran while one was open for 35% -> 0% of each run, Pallas kernels for 0% -> 0%
where the time goes in v1:
time: 153 us; the launch traced here: 152 us
  Pallas kernels  148 us (97%)
  local copies, waits for them, and re-layouts  4.1 us (3%)
    pallas_call x1, Pallas kernels, on_device(): pl.pallas_call(kernel, out_shape=(jax.ShapeDtypeStruct((OUT_ROWS, OUT_COL...  148 us
    unnamed x4, local copies, waits for them, and re-layouts  4.1 us

profile of v1, /device:TPU:1, one launch (start us, length us, event | category | flops | bytes accessed | tf_op | source)
XLA Modules:
  0.0 152.5 jit_solution(711638928218385603)
XLA Ops:
  0.6 147.7 %shard_map.59 = (f32[384,1536]{1,0:T(8,128)}, bf16[768,384]{1,0:T(8,128)(2,1)}) custom-call(f32[1,768,1536]{2,1,0:T(8,128)} %children.1, bf16[1,3,64,1024]{3,2,1,0:T(8,128)(2,1)} %inverse.1, f32[384,1536]{1,0:T(8,128)} %parent.1, s32[2,9216]{1,0:T(2,128)} %child_map.1), custom_call_target="tpu_custom_call" | custom-call | tf_op jit(solution)/shard_map/pallas_call | solution.py:551
  148.3 0.0 copy-start
  148.4 3.3 %copy.8 = f32[384,1536]{1,0:T(8,128)} copy(f32[384,1536]{1,0:T(8,128)} %get-tuple-element.8) | data formatting | bytes 4718592
  151.6 0.0 copy-done
  151.6 0.8 copy.9
Async XLA Ops:
  148.3 3.3 %copy-start = (bf16[768,384]{1,0:T(8,128)(2,1)S(1)}, bf16[768,384]{1,0:T(8,128)(2,1)}, u32[]{:S(2)}) copy-start(bf16[768,384]{1,0:T(8,128)(2,1)} %get-tuple-element.5) | copy-start | bytes 1769476
